TPU v7x, 32 devices: a whole 2x2x4 slice. The times are simulated.
32 devices in a mesh: groups: 2 (over y), sub: 4 (over z), beam: 4 (over x, core).
Axes of the slice: x: 2, y: 2, z: 4, core: 2. Of those that a mesh axis runs over, the one named last changes fastest.
Arguments:
- pulses: float32 [16384, 2, 384], P(('groups', 'sub', 'beam')), parts along dimension 0, may hold values from -6 to 6
- owners: int32 [16384, 1], P(('groups', 'sub', 'beam')), parts along dimension 0, may hold values from 0 to 3; in each aligned block of 512 rows (0 to 511, 512 to 1023, ...) at most 256 rows name the same one
- interp: bfloat16 [2, 2, 4, 2, 128, 128], P(None, None, 'beam'), may hold values from -0.375 to 0.375
- pattern: int32 [2, 4, 2], replicated, may hold values from 0 to 3
Outputs:
- image: bfloat16 [8, 512, 2, 384], P(('groups', 'sub'), 'beam'), parts along dimension 0
There are 2 independent parts, one for each index of `groups`. A program takes and returns all parts, laid end to end along the dimension named above; an argument that names none is the same for every part. Nothing has to cross between parts.
Inputs may be any that keep to these rules, and one draw needn't show every extreme that they name: `owners`: at most 256 of the pulses held by one device name the same owner.
All inputs are finite; a program needn't handle non-finite values.
Results may differ from a plain program's by a relative error of at most 0.0057.
Values may be sent and summed in bfloat16 or wider, within the bound.
A program may use at most 64 MiB of HBM per device.

v0:
```python
import functools
import math

import jax
import jax.numpy as jnp
import numpy as np
from jax import lax
from jax.experimental import pallas as pl
from jax.experimental.pallas import tpu as pltpu
from jax.sharding import PartitionSpec as P

two_pi = 2.0 * math.pi
phase_modulus = 1021


def partner_2(block, axis, bit):
    count = lax.axis_size(axis)
    route = []
    for low in range(count):
        high = low | 1 << bit
        if high != low and high < count:
            route += [(low, high), (high, low)]
    return lax.ppermute(block, axis, route)


def steer_terms(beam_rows, sample_positions, beam_count):
    turns = beam_rows[:, None] * sample_positions[None, :] % beam_count
    angle = turns.astype(jnp.float32) * (two_pi / beam_count)
    return (jnp.cos(angle), jnp.sin(angle))


def beamform(cosine, sine, samples):
    range_len = samples.shape[2]
    flat = samples.reshape(samples.shape[0], 2 * range_len)
    first = jnp.dot(
        cosine, flat, precision=lax.Precision.HIGHEST, preferred_element_type=jnp.float32
    )
    second = jnp.dot(
        sine, flat, precision=lax.Precision.HIGHEST, preferred_element_type=jnp.float32
    )
    first = first.reshape(-1, 2, range_len)
    second = second.reshape(-1, 2, range_len)
    real_part = first[:, 0] + second[:, 1]
    imag_part = first[:, 1] - second[:, 0]
    return jnp.stack([real_part, imag_part], axis=1)


def phase_table(level, half, role, beam_rows, range_len):
    beam_ids = beam_rows[:, None] + 1
    range_ids = jnp.arange(range_len, dtype=jnp.int32)[None, :] + 1
    factor = 4 * level + 2 * half + role + 1
    turns = beam_ids * range_ids * factor % phase_modulus
    angle = turns.astype(jnp.float32) * (two_pi / phase_modulus)
    return (jnp.cos(angle), jnp.sin(angle))


def rotate(term, cosine, sine):
    real_part = cosine * term[:, 0] - sine * term[:, 1]
    imag_part = cosine * term[:, 1] + sine * term[:, 0]
    return jnp.stack([real_part, imag_part], axis=1)


def local_general(pulses, owners, interp, pattern):
    sub_count = lax.axis_size("sub")
    beam_count = lax.axis_size("beam")
    sub_index = lax.axis_index("sub")
    beam_index = lax.axis_index("beam")
    pulse_count = pulses.shape[0]
    range_len = pulses.shape[2]
    levels = interp.shape[0]
    tiles_here = interp.shape[2]
    tile_row_block = interp.shape[-1]
    beam_here = tiles_here * tile_row_block
    beam_total = beam_here * beam_count
    capacity = max(2, 2 * pulse_count // sub_count)
    slot_total = sub_count * capacity
    owner_list = owners[:, 0]
    member = (owner_list[:, None] == jnp.arange(sub_count, dtype=jnp.int32)[None, :]).astype(
        jnp.int32
    )
    earlier = jnp.cumsum(member, axis=0) - member
    slot_rank = jnp.sum(earlier * member, axis=1)
    target = owner_list * capacity + slot_rank
    placing = (target[None, :] == jnp.arange(slot_total, dtype=jnp.int32)[:, None]).astype(
        jnp.float32
    )
    device_rank = sub_index * beam_count + beam_index
    sample_positions = (
        device_rank * pulse_count + jnp.arange(pulse_count, dtype=jnp.int32)
    ).astype(jnp.float32)
    send_samples = jnp.dot(
        placing,
        pulses.reshape(pulse_count, 2 * range_len),
        precision=lax.Precision.HIGHEST,
        preferred_element_type=jnp.float32,
    )
    send_samples = send_samples.reshape(sub_count, capacity, 2, range_len)
    send_positions = jnp.dot(
        placing,
        sample_positions,
        precision=lax.Precision.HIGHEST,
        preferred_element_type=jnp.float32,
    )
    send_positions = send_positions.reshape(sub_count, capacity)
    got_samples, got_positions = (
        lax.all_to_all(send_samples, "sub", split_axis=0, concat_axis=0, tiled=True),
        lax.all_to_all(send_positions, "sub", split_axis=0, concat_axis=0, tiled=True),
    )
    got_samples = got_samples.reshape(slot_total, 2, range_len)
    got_positions = got_positions.reshape(slot_total)
    scale = 1.0 / math.sqrt(pulse_count * beam_count)
    my_rows = beam_index * beam_here + jnp.arange(beam_here, dtype=jnp.int32)
    slot_positions = got_positions.astype(jnp.int32)
    rows = jnp.arange(beam_here * lax.axis_size("beam"), dtype=jnp.int32)
    partial_cosine, partial_sine = steer_terms(rows, slot_positions, beam_total)
    base = lax.psum_scatter(
        beamform(partial_cosine, partial_sine, got_samples), "beam", scatter_dimension=0, tiled=True
    )
    image = (scale * base).astype(jnp.bfloat16)
    for level in range(levels):
        half = sub_index >> level & 1
        local_access_pattern = lax.dynamic_slice_in_dim(
            pattern[level], beam_index * tiles_here, tiles_here, 0
        )
        own_weights = lax.dynamic_index_in_dim(interp[level], half, 0, keepdims=False)
        other_weights = lax.dynamic_index_in_dim(interp[level], 1 - half, 0, keepdims=False)

        def taps_sum(interp_weight_table, piece):
            piece_tiles = piece.reshape(-1, tile_row_block, 2 * range_len)
            tile_count = piece_tiles.shape[0]
            inside = (local_access_pattern >= 0) & (local_access_pattern < tile_count)
            selected_entries = piece_tiles[jnp.clip(local_access_pattern, 0, tile_count - 1)]
            selected_entries = jnp.where(
                inside[:, :, None, None], selected_entries, jnp.zeros((), jnp.bfloat16)
            )
            return jnp.einsum(
                "jvlx,jvxu->jlu",
                interp_weight_table,
                selected_entries,
                preferred_element_type=jnp.float32,
            )

        partner = partner_2(image, "sub", level)
        local_term_value = taps_sum(own_weights, lax.all_gather(image, "beam", axis=0, tiled=True))
        other_term = taps_sum(other_weights, lax.all_gather(partner, "beam", axis=0, tiled=True))
        merged = jnp.zeros((beam_here, 2, range_len), jnp.float32)
        for term_part, role in ((local_term_value, half), (other_term, 1 - half)):
            term = term_part.reshape(beam_here, 2, range_len)
            cosine, sine = phase_table(level, half, role, my_rows, range_len)
            merged = merged + rotate(term, cosine, sine)
        image = merged.astype(jnp.bfloat16)
    return image[None]


MESH = pl.DeviceIdType.MESH


def kernel(
    dims, x_ref, own_ref, interp_ref, pattern_ref, steer_ref, phase_ref, out_ref,
    got, got_own, weights, sums, turns, image, term, send, landed,
    pulse_send, pulse_recv, own_send, own_recv, weight_send, weight_recv, out_send, out_recv,
):
    subs, beams, ranges, tile, levels, scale = dims
    count = subs * beams
    rows = 2 * ranges
    group = lax.axis_index("groups")
    beam = lax.axis_index("beam")
    me = lax.axis_index("sub") * beams + beam

    def place(peer):
        return (group, peer // beams, peer % beams)

    def ahead(step):
        return lax.rem(me + step, count)

    barrier = pltpu.get_barrier_semaphore()
    for step in range(1, count):
        pl.semaphore_signal(barrier, inc=1, device_id=place(ahead(step)), device_id_type=MESH)
    pl.semaphore_wait(barrier, count - 1)

    pulse_copies, own_copies = [None], [None]
    for step in range(1, count):
        own_copy = pltpu.make_async_remote_copy(
            src_ref=own_ref, dst_ref=got_own.at[step],
            send_sem=own_send.at[step], recv_sem=own_recv.at[step],
            device_id=place(ahead(step)), device_id_type=MESH,
        )
        own_copy.start()
        own_copies.append(own_copy)
        copy = pltpu.make_async_remote_copy(
            src_ref=x_ref.at[ahead(step)], dst_ref=got.at[step],
            send_sem=pulse_send.at[step], recv_sem=pulse_recv.at[step],
            device_id=place(ahead(step)), device_id_type=MESH,
        )
        copy.start()
        pulse_copies.append(copy)

    def beam_at(slot):
        return lax.rem(beam // 2 + slot // 2, 2) * 2 + lax.rem(beam % 2 + slot % 2, 2)

    def weight_copy(source, slot, toward):
        return pltpu.make_async_remote_copy(
            src_ref=source, dst_ref=weights.at[slot],
            send_sem=weight_send.at[slot], recv_sem=weight_recv.at[slot],
            device_id=(group, lax.axis_index("sub"), beam_at(toward)), device_id_type=MESH,
        )

    across = weight_copy(interp_ref, 2, 2)
    across.start()
    beside = weight_copy(interp_ref, 1, 1)
    beside.start()

    first_cos = phase_ref[me, 0]
    first_sin = phase_ref[me, 1]
    power_cos, power_sin = first_cos, first_sin
    for power in range(4 * levels):
        if power:
            power_cos, power_sin = (
                power_cos * first_cos - power_sin * first_sin,
                power_cos * first_sin + power_sin * first_cos,
            )
        turns[power, 0] = power_cos
        turns[power, 1] = power_sin

    def add_in(values, owner_row, begin):
        wide = values.astype(jnp.float32)
        for owner in range(subs):
            part = jnp.where(owner_row == owner, wide, 0.0)
            at = pl.ds(owner * rows, rows)
            sums[at, :] = part if begin else sums[at, :] + part

    add_in(x_ref[me], own_ref[...], True)

    across.wait_recv()
    passed_on = weight_copy(weights.at[2], 3, 1)
    passed_on.start()

    for step in range(1, count):
        own_copies[step].wait_recv()
        pulse_copies[step].wait_recv()
        add_in(got[step], got_own[step], False)

    turned = jnp.dot(
        sums[...].astype(jnp.bfloat16), steer_ref[...], preferred_element_type=jnp.float32
    )
    width = turned.shape[1] // 2
    tiles = width // tile

    def members(level, half):
        return [s for s in range(subs) if s >> level & 1 == half]

    def keep(level, owner, block, value):
        half = owner >> level & 1
        at = members(level, half).index(owner) * rows
        image[block, half, at : at + rows, :] = value

    for owner in range(subs):
        part = turned[owner * rows : (owner + 1) * rows]
        real = part[:ranges, :width] + part[ranges:, width:]
        imag = part[ranges:, :width] - part[:ranges, width:]
        base = (scale * jnp.concatenate([real, imag], axis=0)).astype(jnp.bfloat16)
        for block in range(tiles):
            keep(0, owner, block, base[:, block * tile : (block + 1) * tile])

    beside.wait_recv()
    passed_on.wait_recv()

    out_copies = []
    for level in range(levels):
        bit = 1 << level
        for slot in range(tiles):
            block = beam_at(slot)
            for half in range(2):
                value = None
                for tap in range(2):
                    kernel_here = (
                        interp_ref[level, half, 0, tap]
                        if slot == 0
                        else weights[slot, level, half, 0, tap]
                    )
                    child = image[pattern_ref[level, block, tap], half]
                    product = lax.dot_general(
                        child, kernel_here, (((1,), (1,)), ((), ())),
                        preferred_element_type=jnp.float32,
                    )
                    value = product if value is None else value + product
                term[block, half] = value
        for owner in range(subs):
            half = owner >> level & 1
            for block in range(tiles):
                real = imag = 0.0
                for role in range(2):
                    child = owner - half * bit + role * bit
                    at = members(level, role).index(child) * rows
                    power = 4 * level + 2 * half + role
                    lanes = pl.ds(block * tile, tile)
                    cosine = turns[power, 0, :, lanes]
                    sine = turns[power, 1, :, lanes]
                    child_real = term[block, role, at : at + ranges, :]
                    child_imag = term[block, role, at + ranges : at + rows, :]
                    real = real + (cosine * child_real - sine * child_imag)
                    imag = imag + (cosine * child_imag + sine * child_real)
                merged = jnp.concatenate([real, imag], axis=0).astype(jnp.bfloat16)
                if level < levels - 1:
                    keep(level + 1, owner, block, merged)
                else:
                    send[owner * beams + block] = merged

    for step in range(1, count):
        copy = pltpu.make_async_remote_copy(
            src_ref=send.at[ahead(step)], dst_ref=landed.at[step],
            send_sem=out_send.at[step], recv_sem=out_recv.at[step],
            device_id=place(ahead(step)), device_id_type=MESH,
        )
        copy.start()
        out_copies.append(copy)
    out_ref[me] = send[me]
    for step in range(1, count):
        out_copies[step - 1].wait_recv()
        out_ref[lax.rem(me + count - step, count)] = landed[step]
    for step in range(1, count):
        out_copies[step - 1].wait_send()
        pulse_copies[step].wait_send()
        own_copies[step].wait_send()
    across.wait_send()
    beside.wait_send()
    passed_on.wait_send()


def local_sliced(pulses, owners, interp, pattern, *, subs, beams):
    pulse_count, _, range_len = pulses.shape
    levels, _, _, taps, tile, _ = interp.shape
    count = subs * beams
    ranges = range_len // count
    rows = 2 * ranges
    width = beams * tile
    x = pulses.astype(jnp.bfloat16).reshape(pulse_count, 2, count, ranges)
    x = x.transpose(2, 1, 3, 0).reshape(count, rows, pulse_count)
    angle = two_pi / width * (np.arange(pulse_count)[:, None] * np.arange(width)[None, :] % width)
    steer = np.concatenate([np.cos(angle), np.sin(angle)], axis=1).astype(jnp.bfloat16)
    beam_ids = np.arange(width)[None, :] + 1
    range_ids = np.arange(range_len)[:, None] + 1
    phase = two_pi / phase_modulus * (beam_ids * range_ids % phase_modulus)
    phase = np.stack([np.cos(phase), np.sin(phase)], axis=0).astype(np.float32)
    phase = phase.reshape(2, count, ranges, width).transpose(1, 0, 2, 3)
    scale = 1.0 / math.sqrt(pulse_count * beams)
    vmem = pl.BlockSpec(memory_space=pltpu.VMEM)
    out = pl.pallas_call(
        functools.partial(kernel, (subs, beams, ranges, tile, levels, scale)),
        out_shape=jax.ShapeDtypeStruct((count, rows, tile), jnp.bfloat16),
        in_specs=[vmem, vmem, vmem, pl.BlockSpec(memory_space=pltpu.SMEM), vmem, vmem],
        out_specs=vmem,
        scratch_shapes=[
            pltpu.VMEM((count, rows, pulse_count), jnp.bfloat16),
            pltpu.VMEM((count, 1, pulse_count), jnp.int32),
            pltpu.VMEM((4,) + interp.shape, jnp.bfloat16),
            pltpu.VMEM((subs * rows, pulse_count), jnp.float32),
            pltpu.VMEM((4 * levels, 2, ranges, width), jnp.float32),
            pltpu.VMEM((beams, 2, subs // 2 * rows, tile), jnp.bfloat16),
            pltpu.VMEM((beams, 2, subs // 2 * rows, tile), jnp.float32),
            pltpu.VMEM((count, rows, tile), jnp.bfloat16),
            pltpu.VMEM((count, rows, tile), jnp.bfloat16),
        ]
        + [pltpu.SemaphoreType.DMA((count,))] * 4
        + [pltpu.SemaphoreType.DMA((4,))] * 2
        + [pltpu.SemaphoreType.DMA((count,))] * 2,
        compiler_params=pltpu.CompilerParams(
            collective_id=0, has_side_effects=True, vmem_limit_bytes=40 * 2**20
        ),
    )(x, owners.reshape(1, pulse_count), interp, pattern, steer, phase)
    out = out.reshape(count, 2, ranges, tile).transpose(3, 1, 0, 2)
    return out.reshape(1, tile, 2, range_len)


def solution(mesh):
    subs, beams = mesh.shape["sub"], mesh.shape["beam"]

    def local(pulses, owners, interp, pattern):
        pulse_count, _, range_len = pulses.shape
        levels, _, tiles_here, taps, tile, _ = interp.shape
        if (
            range_len % (8 * subs * beams) == 0
            and beams == 4
            and subs == 1 << levels
            and tiles_here == 1
            and taps == 2
            and pulse_count % (beams * tile) == 0
            and tile % 128 == 0
        ):
            return local_sliced(pulses, owners, interp, pattern, subs=subs, beams=beams)
        return local_general(pulses, owners, interp, pattern)

    in_specs = (
        P(("groups", "sub", "beam"), None, None),
        P(("groups", "sub", "beam"), None),
        P(None, None, "beam", None, None, None),
        P(),
    )
    out_specs = P(("groups", "sub"), "beam", None, None)
    return jax.shard_map(local, mesh=mesh, in_specs=in_specs, out_specs=out_specs, check_vma=False)
```

profile of v0, /device:TPU:0, one launch (start us, length us, event | category | flops | bytes accessed | tf_op | source)
XLA Modules:
  0.0 39.7 jit_solution(15263791213897563431)
XLA Ops:
  0.0 0.0 copy-start
  0.0 0.0 copy-start.1
  0.0 0.0 copy-start.4
  0.0 0.0 copy-start.3
  0.0 3.4 %copy.10 = bf16[512,2,384]{0,2,1:T(8,128)(2,1)} copy(f32[512,2,384]{2,1,0:T(2,128)} %param.6) | data formatting | bytes 2359296 | tf_op args[0]
  3.4 1.2 %copy.11 = bf16[16,2,24,512]{3,2,1,0:T(8,128)(2,1)S(1)} copy(bf16[16,2,24,512]{3,2,0,1:T(8,128)(2,1)} %bitcast.12) | data formatting | bytes 1572864 | tf_op jit(solution)/shard_map/transpose | solution.py:338
  4.6 0.0 copy-done.4
  4.6 0.1 copy.12.pattern_ref
  4.7 0.0 copy-done
  4.7 0.0 copy-done.1
  4.8 0.0 copy-done.3
  4.8 0.0 copy-start.2
  4.8 0.9 %copy-done.2 = bf16[2,2,1,2,128,128]{5,4,3,2,1,0:T(8,128)(2,1)S(1)} copy-done((bf16[2,2,1,2,128,128]{5,4,3,2,1,0:T(8,128)(2,1)S(1)}, bf16[2,2,1,2,128,128]{5,4,3,2,1,0:T(8,128)(2,1)}, u32[]{:S(2)}) %copy-start.2) | copy-done | bytes 262168
  5.7 33.1 %shard_map.64 = bf16[16,48,128]{2,1,0:T(8,128)(2,1)S(1)} custom-call(bf16[16,48,512]{2,1,0:T(8,128)(2,1)S(1)} %bitcast.9, s32[1,512]{1,0:T(1,128)S(1)} %bitcast.11, bf16[2,2,1,2,128,128]{5,4,3,2,1,0:T(8,128)(2,1)S(1)} %copy-done.2, s32[2,4,2]{2,1,0:T(4,128)S(1)} %copy.12.pattern_ref, bf16[512,1024]{1,0:T(8,128)(2,1)S(1)} %copy-done.1, ...), custom_call_target="tpu_custom_call" | custom-call | tf_op jit(solution)/shard_map/pallas_call | solution.py:348
  38.9 0.8 %copy.14 = bf16[1,128,2,384]{3,2,1,0:T(2,128)(2,1)} copy(bf16[1,128,2,384]{1,3,2,0:T(8,128)(2,1)S(1)} %bitcast.13) | data formatting | bytes 393216 | tf_op jit(solution)/shard_map/reshape | solution.py:372
  (1 shorter events, 0.0 us)
Async XLA Ops:
  0.0 4.7 %copy-start = (f32[16,2,24,512]{3,2,1,0:T(8,128)S(1)}, f32[16,2,24,512]{3,2,1,0:T(8,128)}, u32[]{:S(2)}) copy-start(f32[16,2,24,512]{3,2,1,0:T(8,128)} %constant.5.clone.phase_ref) | copy-start | bytes 4718596
  0.0 4.7 %copy-start.1 = (bf16[512,1024]{1,0:T(8,128)(2,1)S(1)}, bf16[512,1024]{1,0:T(8,128)(2,1)}, u32[]{:S(2)}) copy-start(bf16[512,1024]{1,0:T(8,128)(2,1)} %constant.4.clone.steer_ref) | copy-start | bytes 3145732
  0.0 4.6 %copy-start.4 = (s32[2,4,2]{1,2,0:T(2,128)S(1)}, s32[2,4,2]{1,2,0:T(2,128)}, u32[]{:S(2)}) copy-start(s32[2,4,2]{1,2,0:T(2,128)} %param.9) | copy-start | bytes 196
  0.0 4.7 %copy-start.3 = (s32[512,1]{0,1:T(1,128)S(1)}, s32[512,1]{0,1:T(1,128)}, u32[]{:S(2)}) copy-start(s32[512,1]{0,1:T(1,128)} %param.7) | copy-start | bytes 6148
  4.8 1.0 %copy-start.2 = (bf16[2,2,1,2,128,128]{5,4,3,2,1,0:T(8,128)(2,1)S(1)}, bf16[2,2,1,2,128,128]{5,4,3,2,1,0:T(8,128)(2,1)}, u32[]{:S(2)}) copy-start(bf16[2,2,1,2,128,128]{5,4,3,2,1,0:T(8,128)(2,1)} %interp_ref.1) | copy-start | bytes 786436
where the time goes:
time: 39.9 us; the launch traced here: 39.7 us
  Pallas kernels  33.1 us (83%)
  local copies, waits for them, and re-layouts  6.55 us (16%)
    pallas_call x1, Pallas kernels, local_sliced(): pl.pallas_call(functools.partial(kernel, (subs, beams, ranges, tile, leve...  33.1 us
    unnamed x12, local copies, waits for them, and re-layouts  4.47 us
    transpose x1, local copies, waits for them, and re-layouts, local_sliced(): x = x.transpose(2, 1, 3, 0).reshape(count, rows, pulse_count)  1.21 us
    reshape x1, local copies, waits for them, and re-layouts, local_sliced(): return out.reshape(1, tile, 2, range_len)  0.85 us

commit v1 on v0

--- a/solution.py
+++ b/solution.py
@@ -156,9 +156,9 @@
 
 
 def kernel(
-    dims, x_ref, own_ref, interp_ref, pattern_ref, steer_ref, phase_ref, out_ref,
-    got, got_own, weights, sums, turns, image, term, send, landed,
-    pulse_send, pulse_recv, own_send, own_recv, weight_send, weight_recv, out_send, out_recv,
+    dims, raw_ref, own_ref, interp_ref, pattern_ref, steer_ref, phase_ref, out_ref,
+    raw, spread, pieces, steer, phase, got, got_own, weights, sums, turns, image, term, send, landed,
+    local_sem, pulse_send, pulse_recv, own_send, own_recv, weight_send, weight_recv, out_send, out_recv,
 ):
     subs, beams, ranges, tile, levels, scale = dims
     count = subs * beams
@@ -176,19 +176,49 @@
     barrier = pltpu.get_barrier_semaphore()
     for step in range(1, count):
         pl.semaphore_signal(barrier, inc=1, device_id=place(ahead(step)), device_id_type=MESH)
+
+    staged = [
+        pltpu.make_async_copy(source, target, local_sem.at[number])
+        for number, (source, target) in enumerate(
+            [
+                (raw_ref, raw),
+                (interp_ref, weights.at[0]),
+                (own_ref, got_own.at[0]),
+                (phase_ref.at[me], phase),
+                (steer_ref, steer),
+            ]
+        )
+    ]
+    for copy in staged:
+        copy.start()
+
+    span = spread.shape[1]
+    lane_tiles = span // 128
+    pulse_count = spread.shape[2]
+    staged[0].wait()
+    for lane_tile in range(lane_tiles):
+        for part in range(2):
+            block = raw[:, part, pl.ds(128 * lane_tile, 128)]
+            spread[part, pl.ds(128 * lane_tile, 128), :] = block.T
+    for piece in range(count):
+        at = pl.ds(piece * ranges, ranges)
+        both = jnp.concatenate([spread[0, at, :], spread[1, at, :]], axis=0)
+        pieces[piece] = both.astype(jnp.bfloat16)
+    for copy in staged[1:]:
+        copy.wait()
     pl.semaphore_wait(barrier, count - 1)
 
     pulse_copies, own_copies = [None], [None]
     for step in range(1, count):
         own_copy = pltpu.make_async_remote_copy(
-            src_ref=own_ref, dst_ref=got_own.at[step],
+            src_ref=got_own.at[0], dst_ref=got_own.at[step],
             send_sem=own_send.at[step], recv_sem=own_recv.at[step],
             device_id=place(ahead(step)), device_id_type=MESH,
         )
         own_copy.start()
         own_copies.append(own_copy)
         copy = pltpu.make_async_remote_copy(
-            src_ref=x_ref.at[ahead(step)], dst_ref=got.at[step],
+            src_ref=pieces.at[ahead(step)], dst_ref=got.at[step],
             send_sem=pulse_send.at[step], recv_sem=pulse_recv.at[step],
             device_id=place(ahead(step)), device_id_type=MESH,
         )
@@ -205,13 +235,13 @@
             device_id=(group, lax.axis_index("sub"), beam_at(toward)), device_id_type=MESH,
         )
 
-    across = weight_copy(interp_ref, 2, 2)
+    across = weight_copy(weights.at[0], 2, 2)
     across.start()
-    beside = weight_copy(interp_ref, 1, 1)
+    beside = weight_copy(weights.at[0], 1, 1)
     beside.start()
 
-    first_cos = phase_ref[me, 0]
-    first_sin = phase_ref[me, 1]
+    first_cos = phase[0]
+    first_sin = phase[1]
     power_cos, power_sin = first_cos, first_sin
     for power in range(4 * levels):
         if power:
@@ -229,7 +259,7 @@
             at = pl.ds(owner * rows, rows)
             sums[at, :] = part if begin else sums[at, :] + part
 
-    add_in(x_ref[me], own_ref[...], True)
+    add_in(pieces[me], got_own[0], True)
 
     across.wait_recv()
     passed_on = weight_copy(weights.at[2], 3, 1)
@@ -241,7 +271,7 @@
         add_in(got[step], got_own[step], False)
 
     turned = jnp.dot(
-        sums[...].astype(jnp.bfloat16), steer_ref[...], preferred_element_type=jnp.float32
+        sums[...].astype(jnp.bfloat16), steer[...], preferred_element_type=jnp.float32
     )
     width = turned.shape[1] // 2
     tiles = width // tile
@@ -273,12 +303,8 @@
             for half in range(2):
                 value = None
                 for tap in range(2):
-                    kernel_here = (
-                        interp_ref[level, half, 0, tap]
-                        if slot == 0
-                        else weights[slot, level, half, 0, tap]
-                    )
-                    child = image[pattern_ref[level, block, tap], half]
+                    kernel_here = weights[slot, level, half, 0, tap]
+                    child = image[pattern_ref[level, tap, block], half]
                     product = lax.dot_general(
                         child, kernel_here, (((1,), (1,)), ((), ())),
                         preferred_element_type=jnp.float32,
@@ -308,16 +334,24 @@
 
     for step in range(1, count):
         copy = pltpu.make_async_remote_copy(
-            src_ref=send.at[ahead(step)], dst_ref=landed.at[step],
-            send_sem=out_send.at[step], recv_sem=out_recv.at[step],
+            src_ref=send.at[ahead(step)], dst_ref=landed.at[me],
+            send_sem=out_send.at[step], recv_sem=out_recv.at[me],
             device_id=place(ahead(step)), device_id_type=MESH,
         )
         copy.start()
         out_copies.append(copy)
-    out_ref[me] = send[me]
-    for step in range(1, count):
-        out_copies[step - 1].wait_recv()
-        out_ref[lax.rem(me + count - step, count)] = landed[step]
+    landed[me] = send[me]
+    for step in range(1, count):
+        source = ahead(count - step)
+        pltpu.make_async_remote_copy(
+            src_ref=send.at[source], dst_ref=landed.at[source],
+            send_sem=out_send.at[step], recv_sem=out_recv.at[source],
+            device_id=place(source), device_id_type=MESH,
+        ).wait_recv()
+    for part in range(2):
+        strips = [landed[source].astype(jnp.float32) for source in range(count)]
+        whole = [strip[part * ranges : (part + 1) * ranges] for strip in strips]
+        out_ref[part] = jnp.concatenate(whole, axis=0).astype(jnp.bfloat16)
     for step in range(1, count):
         out_copies[step - 1].wait_send()
         pulse_copies[step].wait_send()
@@ -334,8 +368,7 @@
     ranges = range_len // count
     rows = 2 * ranges
     width = beams * tile
-    x = pulses.astype(jnp.bfloat16).reshape(pulse_count, 2, count, ranges)
-    x = x.transpose(2, 1, 3, 0).reshape(count, rows, pulse_count)
+    x = pulses
     angle = two_pi / width * (np.arange(pulse_count)[:, None] * np.arange(width)[None, :] % width)
     steer = np.concatenate([np.cos(angle), np.sin(angle)], axis=1).astype(jnp.bfloat16)
     beam_ids = np.arange(width)[None, :] + 1
@@ -345,12 +378,18 @@
     phase = phase.reshape(2, count, ranges, width).transpose(1, 0, 2, 3)
     scale = 1.0 / math.sqrt(pulse_count * beams)
     vmem = pl.BlockSpec(memory_space=pltpu.VMEM)
+    hbm = pl.BlockSpec(memory_space=pltpu.HBM)
     out = pl.pallas_call(
         functools.partial(kernel, (subs, beams, ranges, tile, levels, scale)),
-        out_shape=jax.ShapeDtypeStruct((count, rows, tile), jnp.bfloat16),
-        in_specs=[vmem, vmem, vmem, pl.BlockSpec(memory_space=pltpu.SMEM), vmem, vmem],
+        out_shape=jax.ShapeDtypeStruct((2, range_len, tile), jnp.bfloat16),
+        in_specs=[hbm, hbm, hbm, pl.BlockSpec(memory_space=pltpu.SMEM), hbm, hbm],
         out_specs=vmem,
         scratch_shapes=[
+            pltpu.VMEM(x.shape, jnp.float32),
+            pltpu.VMEM((2, range_len, pulse_count), jnp.float32),
+            pltpu.VMEM((count, rows, pulse_count), jnp.bfloat16),
+            pltpu.VMEM(steer.shape, jnp.bfloat16),
+            pltpu.VMEM(phase.shape[1:], jnp.float32),
             pltpu.VMEM((count, rows, pulse_count), jnp.bfloat16),
             pltpu.VMEM((count, 1, pulse_count), jnp.int32),
             pltpu.VMEM((4,) + interp.shape, jnp.bfloat16),
@@ -361,15 +400,15 @@
             pltpu.VMEM((count, rows, tile), jnp.bfloat16),
             pltpu.VMEM((count, rows, tile), jnp.bfloat16),
         ]
+        + [pltpu.SemaphoreType.DMA((5,))]
         + [pltpu.SemaphoreType.DMA((count,))] * 4
         + [pltpu.SemaphoreType.DMA((4,))] * 2
         + [pltpu.SemaphoreType.DMA((count,))] * 2,
         compiler_params=pltpu.CompilerParams(
-            collective_id=0, has_side_effects=True, vmem_limit_bytes=40 * 2**20
+            collective_id=0, has_side_effects=True, vmem_limit_bytes=62 * 2**20
         ),
-    )(x, owners.reshape(1, pulse_count), interp, pattern, steer, phase)
-    out = out.reshape(count, 2, ranges, tile).transpose(3, 1, 0, 2)
-    return out.reshape(1, tile, 2, range_len)
+    )(x, owners.reshape(1, pulse_count), interp, pattern.transpose(0, 2, 1), steer, phase)
+    return out.transpose(2, 0, 1)[None]
 
 
 def solution(mesh):
@@ -380,6 +419,7 @@
         levels, _, tiles_here, taps, tile, _ = interp.shape
         if (
             range_len % (8 * subs * beams) == 0
+            and range_len % 128 == 0
             and beams == 4
             and subs == 1 << levels
             and tiles_here == 1

time: 39.9 us -> 35.9 us (0.90)
  local copies, waits for them, and re-layouts: 6.55 us -> 1.76 us
  Pallas kernels: 33.1 us -> 33.9 us
    unnamed x12 -> x0, local copies, waits for them, and re-layouts: 4.47 us -> none
    broadcast_in_dim x0 -> x1, local copies, waits for them, and re-layouts: none -> 1.76 us  [local_sliced(): return out.transpose(2, 0, 1)[None]]
    transpose x1 -> x0, local copies, waits for them, and re-layouts: 1.21 us -> none  [local_sliced(): x = x.transpose(2, 1, 3, 0).reshape(count, rows, pulse_count)]
    reshape x2 -> x0, local copies, waits for them, and re-layouts: 0.87 us -> none  [the longest x1 0.85 us: local_sliced(): return out.reshape(1, tile, 2, range_len)]
    pallas_call x1, Pallas kernels: 33.1 us -> 33.9 us  [local_sliced(): pl.pallas_call(functools.partial(kernel, (subs, beams, ranges, tile, leve...]
where the time goes in v1:
time: 35.9 us; the launch traced here: 35.7 us
  Pallas kernels  33.9 us (94%)
  local copies, waits for them, and re-layouts  1.76 us (5%)
    pallas_call x1, Pallas kernels, local_sliced(): pl.pallas_call(functools.partial(kernel, (subs, beams, ranges, tile, leve...  33.9 us
    broadcast_in_dim x1, local copies, waits for them, and re-layouts, local_sliced(): return out.transpose(2, 0, 1)[None]  1.76 us

profile of v1, /device:TPU:0, one launch (start us, length us, event | category | flops | bytes accessed | tf_op | source)
XLA Modules:
  0.0 35.7 jit_solution(3829043625690314978)
XLA Ops:
  0.0 33.9 %shard_map.64 = bf16[2,384,128]{2,1,0:T(8,128)(2,1)} custom-call(f32[512,2,384]{2,1,0:T(2,128)} %raw_ref.1, s32[1,512]{1,0:T(1,128)} %bitcast.6, bf16[2,2,1,2,128,128]{5,4,3,2,1,0:T(8,128)(2,1)} %interp_ref.1, s32[2,2,4]{2,1,0:T(2,128)} %bitcast.7, bf16[512,1024]{1,0:T(8,128)(2,1)} %constant.4.clone.steer_ref, f32[16,2,24,512]{3,2,1,0:T(8,128)} %constant.5.clone.phase_ref), custom_call_target="tpu_custom_call" | custom-call | tf_op jit(solution)/shard_map/pallas_call | solution.py:382
  34.0 1.8 %copy.7 = bf16[1,128,2,384]{3,2,1,0:T(2,128)(2,1)} copy(bf16[1,128,2,384]{1,3,2,0:T(8,128)(2,1)} %bitcast.5) | data formatting | bytes 393216 | tf_op jit(solution)/shard_map/broadcast_in_dim | solution.py:411

commit v2 on v1

--- a/solution.py
+++ b/solution.py
@@ -157,8 +157,8 @@
 
 def kernel(
     dims, raw_ref, own_ref, interp_ref, pattern_ref, steer_ref, phase_ref, out_ref,
-    raw, spread, pieces, steer, phase, got, got_own, weights, sums, turns, image, term, send, landed,
-    local_sem, pulse_send, pulse_recv, own_send, own_recv, weight_send, weight_recv, out_send, out_recv,
+    raw, spread, pieces, steer, phase, got, got_own, weights, sums, far_sums, far_out, far_in, summed, turns, image, term, send, landed,
+    local_sem, pulse_send, pulse_recv, own_send, own_recv, weight_send, weight_recv, out_send, out_recv, sum_send, sum_recv,
 ):
     subs, beams, ranges, tile, levels, scale = dims
     count = subs * beams
@@ -208,22 +208,37 @@
         copy.wait()
     pl.semaphore_wait(barrier, count - 1)
 
-    pulse_copies, own_copies = [None], [None]
-    for step in range(1, count):
+    half_count = count // 2
+    base_peer = me // half_count * half_count
+    far = ahead(half_count)
+    far_base = half_count - base_peer
+
+    def beside_me(step):
+        return lax.rem(me - base_peer + step, half_count)
+
+    def pulse_copy(piece, slot, peer):
+        return pltpu.make_async_remote_copy(
+            src_ref=pieces.at[piece], dst_ref=got.at[slot],
+            send_sem=pulse_send.at[slot], recv_sem=pulse_recv.at[slot],
+            device_id=place(peer), device_id_type=MESH,
+        )
+
+    own_copies, far_copies, near_copies = [None], [None], [None]
+    for step in range(1, half_count):
+        peer = base_peer + beside_me(step)
         own_copy = pltpu.make_async_remote_copy(
             src_ref=got_own.at[0], dst_ref=got_own.at[step],
             send_sem=own_send.at[step], recv_sem=own_recv.at[step],
-            device_id=place(ahead(step)), device_id_type=MESH,
+            device_id=place(peer), device_id_type=MESH,
         )
         own_copy.start()
         own_copies.append(own_copy)
-        copy = pltpu.make_async_remote_copy(
-            src_ref=pieces.at[ahead(step)], dst_ref=got.at[step],
-            send_sem=pulse_send.at[step], recv_sem=pulse_recv.at[step],
-            device_id=place(ahead(step)), device_id_type=MESH,
-        )
-        copy.start()
-        pulse_copies.append(copy)
+        far_copies.append(pulse_copy(far_base + beside_me(step), step, peer))
+        far_copies[step].start()
+    for step in range(1, half_count):
+        peer = base_peer + beside_me(step)
+        near_copies.append(pulse_copy(peer, half_count + step, peer))
+        near_copies[step].start()
 
     def beam_at(slot):
         return lax.rem(beam // 2 + slot // 2, 2) * 2 + lax.rem(beam % 2 + slot % 2, 2)
@@ -252,27 +267,43 @@
         turns[power, 0] = power_cos
         turns[power, 1] = power_sin
 
-    def add_in(values, owner_row, begin):
+    def add_in(total, values, owner_row, begin):
         wide = values.astype(jnp.float32)
         for owner in range(subs):
             part = jnp.where(owner_row == owner, wide, 0.0)
-            at = pl.ds(owner * rows, rows)
-            sums[at, :] = part if begin else sums[at, :] + part
-
-    add_in(pieces[me], got_own[0], True)
+            total[owner] = part if begin else total[owner] + part
+
+    add_in(far_sums, pieces[far], got_own[0], True)
+    for step in range(1, half_count):
+        own_copies[step].wait_recv()
+        far_copies[step].wait_recv()
+        add_in(far_sums, got[step], got_own[step], False)
+    sum_copies = []
+    for owner in range(subs):
+        far_out[owner] = far_sums[owner].astype(jnp.bfloat16)
+        sum_copy = pltpu.make_async_remote_copy(
+            src_ref=far_out.at[owner], dst_ref=far_in.at[owner],
+            send_sem=sum_send.at[owner], recv_sem=sum_recv.at[owner],
+            device_id=place(far), device_id_type=MESH,
+        )
+        sum_copy.start()
+        sum_copies.append(sum_copy)
+    add_in(sums, pieces[me], got_own[0], True)
 
     across.wait_recv()
     passed_on = weight_copy(weights.at[2], 3, 1)
     passed_on.start()
 
-    for step in range(1, count):
-        own_copies[step].wait_recv()
-        pulse_copies[step].wait_recv()
-        add_in(got[step], got_own[step], False)
-
-    turned = jnp.dot(
-        sums[...].astype(jnp.bfloat16), steer[...], preferred_element_type=jnp.float32
-    )
+    for step in range(1, half_count):
+        near_copies[step].wait_recv()
+        add_in(sums, got[half_count + step], got_own[step], False)
+    for owner in range(subs):
+        sum_copies[owner].wait_recv()
+        summed[pl.ds(owner * rows, rows), :] = (
+            sums[owner] + far_in[owner].astype(jnp.float32)
+        ).astype(jnp.bfloat16)
+
+    turned = jnp.dot(summed[...], steer[...], preferred_element_type=jnp.float32)
     width = turned.shape[1] // 2
     tiles = width // tile
 
@@ -351,11 +382,15 @@
     for part in range(2):
         strips = [landed[source].astype(jnp.float32) for source in range(count)]
         whole = [strip[part * ranges : (part + 1) * ranges] for strip in strips]
-        out_ref[part] = jnp.concatenate(whole, axis=0).astype(jnp.bfloat16)
+        out_ref[part] = jnp.concatenate(whole, axis=0).T.astype(jnp.bfloat16)
     for step in range(1, count):
         out_copies[step - 1].wait_send()
-        pulse_copies[step].wait_send()
+    for step in range(1, half_count):
         own_copies[step].wait_send()
+        far_copies[step].wait_send()
+        near_copies[step].wait_send()
+    for owner in range(subs):
+        sum_copies[owner].wait_send()
     across.wait_send()
     beside.wait_send()
     passed_on.wait_send()
@@ -381,7 +416,7 @@
     hbm = pl.BlockSpec(memory_space=pltpu.HBM)
     out = pl.pallas_call(
         functools.partial(kernel, (subs, beams, ranges, tile, levels, scale)),
-        out_shape=jax.ShapeDtypeStruct((2, range_len, tile), jnp.bfloat16),
+        out_shape=jax.ShapeDtypeStruct((2, tile, range_len), jnp.bfloat16),
         in_specs=[hbm, hbm, hbm, pl.BlockSpec(memory_space=pltpu.SMEM), hbm, hbm],
         out_specs=vmem,
         scratch_shapes=[
@@ -393,7 +428,11 @@
             pltpu.VMEM((count, rows, pulse_count), jnp.bfloat16),
             pltpu.VMEM((count, 1, pulse_count), jnp.int32),
             pltpu.VMEM((4,) + interp.shape, jnp.bfloat16),
-            pltpu.VMEM((subs * rows, pulse_count), jnp.float32),
+            pltpu.VMEM((subs, rows, pulse_count), jnp.float32),
+            pltpu.VMEM((subs, rows, pulse_count), jnp.float32),
+            pltpu.VMEM((subs, rows, pulse_count), jnp.bfloat16),
+            pltpu.VMEM((subs, rows, pulse_count), jnp.bfloat16),
+            pltpu.VMEM((subs * rows, pulse_count), jnp.bfloat16),
             pltpu.VMEM((4 * levels, 2, ranges, width), jnp.float32),
             pltpu.VMEM((beams, 2, subs // 2 * rows, tile), jnp.bfloat16),
             pltpu.VMEM((beams, 2, subs // 2 * rows, tile), jnp.float32),
@@ -403,12 +442,13 @@
         + [pltpu.SemaphoreType.DMA((5,))]
         + [pltpu.SemaphoreType.DMA((count,))] * 4
         + [pltpu.SemaphoreType.DMA((4,))] * 2
-        + [pltpu.SemaphoreType.DMA((count,))] * 2,
+        + [pltpu.SemaphoreType.DMA((count,))] * 2
+        + [pltpu.SemaphoreType.DMA((subs,))] * 2,
         compiler_params=pltpu.CompilerParams(
             collective_id=0, has_side_effects=True, vmem_limit_bytes=62 * 2**20
         ),
     )(x, owners.reshape(1, pulse_count), interp, pattern.transpose(0, 2, 1), steer, phase)
-    return out.transpose(2, 0, 1)[None]
+    return out.transpose(1, 0, 2)[None]
 
 
 def solution(mesh):

time: 35.9 us -> 34.1 us (0.950)
  Pallas kernels: 33.9 us -> 32.1 us
    pallas_call x1, Pallas kernels: 33.9 us -> 32.1 us  [local_sliced(): pl.pallas_call(functools.partial(kernel, (subs, beams, ranges, tile, leve...]
where the time goes in v2:
time: 34.1 us; the launch traced here: 33.9 us
  Pallas kernels  32.1 us (94%)
  local copies, waits for them, and re-layouts  1.81 us (5%)
    pallas_call x1, Pallas kernels, local_sliced(): pl.pallas_call(functools.partial(kernel, (subs, beams, ranges, tile, leve...  32.1 us
    broadcast_in_dim x1, local copies, waits for them, and re-layouts, local_sliced(): return out.transpose(1, 0, 2)[None]  1.81 us

profile of v2, /device:TPU:0, one launch (start us, length us, event | category | flops | bytes accessed | tf_op | source)
XLA Modules:
  0.0 33.9 jit_solution(4996715658558144638)
XLA Ops:
  0.0 32.1 %shard_map.64 = bf16[2,128,384]{2,1,0:T(8,128)(2,1)} custom-call(f32[512,2,384]{2,1,0:T(2,128)} %raw_ref.1, s32[1,512]{1,0:T(1,128)} %bitcast.6, bf16[2,2,1,2,128,128]{5,4,3,2,1,0:T(8,128)(2,1)} %interp_ref.1, s32[2,2,4]{2,1,0:T(2,128)} %bitcast.7, bf16[512,1024]{1,0:T(8,128)(2,1)} %constant.4.clone.steer_ref, f32[16,2,24,512]{3,2,1,0:T(8,128)} %constant.5.clone.phase_ref), custom_call_target="tpu_custom_call" | custom-call | tf_op jit(solution)/shard_map/pallas_call | solution.py:417
  32.1 1.8 %copy.7 = bf16[1,128,2,384]{3,2,1,0:T(2,128)(2,1)} copy(bf16[1,128,2,384]{3,1,2,0:T(8,128)(2,1)} %bitcast.5) | data formatting | bytes 393216 | tf_op jit(solution)/shard_map/broadcast_in_dim | solution.py:451

commit v3 on v2

--- a/solution.py
+++ b/solution.py
@@ -445,7 +445,7 @@
         + [pltpu.SemaphoreType.DMA((count,))] * 2
         + [pltpu.SemaphoreType.DMA((subs,))] * 2,
         compiler_params=pltpu.CompilerParams(
-            collective_id=0, has_side_effects=True, vmem_limit_bytes=62 * 2**20
+            collective_id=0, has_side_effects=True, vmem_limit_bytes=107 * 2**19
         ),
     )(x, owners.reshape(1, pulse_count), interp, pattern.transpose(0, 2, 1), steer, phase)
     return out.transpose(1, 0, 2)[None]

time: 34.1 us -> 33.8 us (level)
  Pallas kernels: 32.1 us -> 31.3 us
  local copies, waits for them, and re-layouts: 1.81 us -> 2.24 us
    unnamed x0 -> x4, local copies, waits for them, and re-layouts: none -> 1.36 us
    broadcast_in_dim x1, local copies, waits for them, and re-layouts: 1.81 us -> 0.88 us  [local_sliced(): return out.transpose(1, 0, 2)[None]]
    pallas_call x1, Pallas kernels: 32.1 us -> 31.3 us  [local_sliced(): pl.pallas_call(functools.partial(kernel, (subs, beams, ranges, tile, leve...]
where the time goes in v3:
time: 33.8 us; the launch traced here: 33.6 us
  Pallas kernels  31.3 us (93%)
  local copies, waits for them, and re-layouts  2.24 us (7%)
    pallas_call x1, Pallas kernels, local_sliced(): pl.pallas_call(functools.partial(kernel, (subs, beams, ranges, tile, leve...  31.3 us
    unnamed x4, local copies, waits for them, and re-layouts  1.36 us
    broadcast_in_dim x1, local copies, waits for them, and re-layouts, local_sliced(): return out.transpose(1, 0, 2)[None]  0.88 us

profile of v3, /device:TPU:0, one launch (start us, length us, event | category | flops | bytes accessed | tf_op | source)
XLA Modules:
  0.0 33.6 jit_solution(5310827182344357439)
XLA Ops:
  0.0 0.0 copy-start
  0.0 0.7 %copy-done = s32[512,1]{0,1:T(1,128)S(1)} copy-done((s32[512,1]{0,1:T(1,128)S(1)}, s32[512,1]{0,1:T(1,128)}, u32[]{:S(2)}) %copy-start) | copy-done | bytes 2072
  0.7 0.0 copy-start.1
  0.7 0.7 %copy-done.1 = s32[2,4,2]{1,2,0:T(2,128)S(1)} copy-done((s32[2,4,2]{1,2,0:T(2,128)S(1)}, s32[2,4,2]{1,2,0:T(2,128)}, u32[]{:S(2)}) %copy-start.1) | copy-done | bytes 88
  1.4 31.3 %shard_map.64 = bf16[2,128,384]{2,1,0:T(8,128)(2,1)S(1)} custom-call(f32[512,2,384]{2,1,0:T(2,128)} %raw_ref.1, s32[1,512]{1,0:T(1,128)S(1)} %bitcast.6, bf16[2,2,1,2,128,128]{5,4,3,2,1,0:T(8,128)(2,1)} %interp_ref.1, s32[2,2,4]{2,1,0:T(2,128)S(1)} %bitcast.7, bf16[512,1024]{1,0:T(8,128)(2,1)} %constant.4.clone.steer_ref, ...), custom_call_target="tpu_custom_call" | custom-call | tf_op jit(solution)/shard_map/pallas_call | solution.py:417
  32.7 0.9 %copy.7 = bf16[1,128,2,384]{3,2,1,0:T(2,128)(2,1)} copy(bf16[1,128,2,384]{3,1,2,0:T(8,128)(2,1)S(1)} %bitcast.5) | data formatting | bytes 393216 | tf_op jit(solution)/shard_map/broadcast_in_dim | solution.py:451
Async XLA Ops:
  0.0 0.7 %copy-start = (s32[512,1]{0,1:T(1,128)S(1)}, s32[512,1]{0,1:T(1,128)}, u32[]{:S(2)}) copy-start(s32[512,1]{0,1:T(1,128)} %param.7) | copy-start | bytes 6148
  0.7 0.7 %copy-start.1 = (s32[2,4,2]{1,2,0:T(2,128)S(1)}, s32[2,4,2]{1,2,0:T(2,128)}, u32[]{:S(2)}) copy-start(s32[2,4,2]{1,2,0:T(2,128)} %param.9) | copy-start | bytes 196

commit v4 on v3

--- a/solution.py
+++ b/solution.py
@@ -326,7 +326,18 @@
     beside.wait_recv()
     passed_on.wait_recv()
 
-    out_copies = []
+    def out_copy(peer):
+        return pltpu.make_async_remote_copy(
+            src_ref=send.at[peer], dst_ref=landed.at[me],
+            send_sem=out_send.at[peer], recv_sem=out_recv.at[me],
+            device_id=place(peer), device_id_type=MESH,
+        )
+
+    def ready(peer):
+        @pl.when(peer != me)
+        def _():
+            out_copy(peer).start()
+
     for level in range(levels):
         bit = 1 << level
         for slot in range(tiles):
@@ -362,21 +373,14 @@
                     keep(level + 1, owner, block, merged)
                 else:
                     send[owner * beams + block] = merged
-
-    for step in range(1, count):
-        copy = pltpu.make_async_remote_copy(
-            src_ref=send.at[ahead(step)], dst_ref=landed.at[me],
-            send_sem=out_send.at[step], recv_sem=out_recv.at[me],
-            device_id=place(ahead(step)), device_id_type=MESH,
-        )
-        copy.start()
-        out_copies.append(copy)
+                    ready(owner * beams + block)
+
     landed[me] = send[me]
     for step in range(1, count):
         source = ahead(count - step)
         pltpu.make_async_remote_copy(
             src_ref=send.at[source], dst_ref=landed.at[source],
-            send_sem=out_send.at[step], recv_sem=out_recv.at[source],
+            send_sem=out_send.at[source], recv_sem=out_recv.at[source],
             device_id=place(source), device_id_type=MESH,
         ).wait_recv()
     for part in range(2):
@@ -384,7 +388,7 @@
         whole = [strip[part * ranges : (part + 1) * ranges] for strip in strips]
         out_ref[part] = jnp.concatenate(whole, axis=0).T.astype(jnp.bfloat16)
     for step in range(1, count):
-        out_copies[step - 1].wait_send()
+        out_copy(ahead(step)).wait_send()
     for step in range(1, half_count):
         own_copies[step].wait_send()
         far_copies[step].wait_send()

time: 33.8 us -> 33.7 us (level)
  no operation moved by 1% of the time
where the time goes in v4:
time: 33.7 us; the launch traced here: 33.5 us
  Pallas kernels  31.2 us (93%)
  local copies, waits for them, and re-layouts  2.24 us (7%)
    pallas_call x1, Pallas kernels, local_sliced(): pl.pallas_call(functools.partial(kernel, (subs, beams, ranges, tile, leve...  31.2 us
    unnamed x4, local copies, waits for them, and re-layouts  1.36 us
    broadcast_in_dim x1, local copies, waits for them, and re-layouts, local_sliced(): return out.transpose(1, 0, 2)[None]  0.88 us

profile of v4, /device:TPU:0, one launch (start us, length us, event | category | flops | bytes accessed | tf_op | source)
XLA Modules:
  0.0 33.5 jit_solution(11063070509157635257)
XLA Ops:
  0.0 0.0 copy-start
  0.0 0.7 %copy-done = s32[512,1]{0,1:T(1,128)S(1)} copy-done((s32[512,1]{0,1:T(1,128)S(1)}, s32[512,1]{0,1:T(1,128)}, u32[]{:S(2)}) %copy-start) | copy-done | bytes 2072
  0.7 0.0 copy-start.1
  0.7 0.7 %copy-done.1 = s32[2,4,2]{1,2,0:T(2,128)S(1)} copy-done((s32[2,4,2]{1,2,0:T(2,128)S(1)}, s32[2,4,2]{1,2,0:T(2,128)}, u32[]{:S(2)}) %copy-start.1) | copy-done | bytes 88
  1.4 31.2 %shard_map.64 = bf16[2,128,384]{2,1,0:T(8,128)(2,1)S(1)} custom-call(f32[512,2,384]{2,1,0:T(2,128)} %raw_ref.1, s32[1,512]{1,0:T(1,128)S(1)} %bitcast.6, bf16[2,2,1,2,128,128]{5,4,3,2,1,0:T(8,128)(2,1)} %interp_ref.1, s32[2,2,4]{2,1,0:T(2,128)S(1)} %bitcast.7, bf16[512,1024]{1,0:T(8,128)(2,1)} %constant.4.clone.steer_ref, ...), custom_call_target="tpu_custom_call" | custom-call | tf_op jit(solution)/shard_map/pallas_call | solution.py:421
  32.6 0.9 %copy.7 = bf16[1,128,2,384]{3,2,1,0:T(2,128)(2,1)} copy(bf16[1,128,2,384]{3,1,2,0:T(8,128)(2,1)S(1)} %bitcast.5) | data formatting | bytes 393216 | tf_op jit(solution)/shard_map/broadcast_in_dim | solution.py:455
Async XLA Ops:
  0.0 0.7 %copy-start = (s32[512,1]{0,1:T(1,128)S(1)}, s32[512,1]{0,1:T(1,128)}, u32[]{:S(2)}) copy-start(s32[512,1]{0,1:T(1,128)} %param.7) | copy-start | bytes 6148
  0.7 0.7 %copy-start.1 = (s32[2,4,2]{1,2,0:T(2,128)S(1)}, s32[2,4,2]{1,2,0:T(2,128)}, u32[]{:S(2)}) copy-start(s32[2,4,2]{1,2,0:T(2,128)} %param.9) | copy-start | bytes 196
